TPU v7x, 32 devices: a whole 2x2x4 slice. The times are simulated.
32 devices in a mesh: row: 8 (over z, x), col: 4 (over y, core).
Axes of the slice: x: 2, y: 2, z: 4, core: 2. Of those that a mesh axis runs over, the one named last changes fastest.
Arguments:
- initial_estimate0: float32 [96, 128, 1024], P(None, 'row', 'col'), may hold values from 0.1 to 1
- clutter: float32 [128, 1024], P('row', 'col'), may hold values from 0 to 1.5
- counts: int32 [32, 96, 128], P(('row', 'col')), may hold values from 1 to 10000
- antenna_settings: float32 [32, 5, 128], P(('row', 'col')), as said below
- tile_block_list: int32 [8, 4, 32], P('row', 'col'), may hold values from 0 to 31, as said below
- tile_block_count: int32 [8, 4], P('row', 'col'), may hold values from 1 to 32
Outputs:
- estimate: float32 [96, 128, 1024], P(None, 'row', 'col')
Inputs may be any that keep to these rules, and one draw needn't show every extreme that they name: `tile_block_list`: block b's owner group along row is b // 4; entry i of a tile's list is used only when i < tile_block_count, and unused entries hold 0; the listed blocks of one tile are distinct; every block is listed by some tile; one tile lists at most 4 blocks of one owner group, and the tiles of some column list 32 blocks each. `antenna_settings`: radii and gains are positive.
All inputs are finite; a program needn't handle non-finite values.
Results may differ from a plain program's by a relative error of at most 0.0003.
Values sent between devices are 32-bit elements; how exact they have to be, the bound alone decides.
A program may use at most 64 MiB of HBM per device.

v0:
```python
import jax
import jax.numpy as jnp
from jax import lax
from jax.experimental import pallas as pl
from jax.experimental.pallas import tpu as pltpu
from jax.sharding import PartitionSpec as P

ITERS = 2
GROUP = 4
CHUNK = 512
LOG2E = 1.4426950408889634
NT = (((1,), (1,)), ((), ()))
VMEM = 50 << 20


def cover_kernel(
    meta, settings, clutter, estimate, cover, partial, column_term, slope, shift, inverse, total
):
    slots, rows, columns = meta.shape[0] - 3, clutter.shape[0], clutter.shape[2]
    antennas = settings.shape[2]
    step = pl.program_id(0)
    wide = (antennas, 128)

    @pl.when(step == 0)
    def _():
        partial[...] = jnp.zeros_like(partial)

    row_start = meta[slots + 1].astype(jnp.float32) + 0.5
    column_start = meta[slots + 2].astype(jnp.float32) + 0.5
    lanes = lax.broadcasted_iota(jnp.int32, wide, 1).astype(jnp.float32)
    for s in range(GROUP):
        here = slice(s * antennas, (s + 1) * antennas)
        record = jnp.transpose(settings[meta[step * GROUP + s]])
        inv = jnp.broadcast_to(1.0 / record[:, 2:3], wide)
        inverse[here, :] = inv
        shift[here, :] = (row_start - jnp.broadcast_to(record[:, 0:1], wide)) * inv
        slope[here, :] = jnp.broadcast_to(record[:, 4:5] * (-LOG2E), wide)
        position = jnp.broadcast_to(record[:, 1:2], wide)
        for h in range(columns // 128):
            d = (lanes + (column_start + h * 128.0) - position) * inv
            column_term[here, h * 128 : (h + 1) * 128] = 1.0 + d * d
    total[...] = jnp.zeros_like(total)

    def row(i, carry):
        base = pl.multiple_of(i * columns, columns)
        offset = i.astype(jnp.float32)
        for s in range(GROUP):
            here = slice(s * antennas, (s + 1) * antennas)
            d = shift[here, :] + offset * inverse[here, :]
            dd = d * d
            k = slope[here, :]
            for h in range(columns // 128):
                loss = clutter[i, :, h * 128 : (h + 1) * 128]
                c = jnp.exp2(k * loss) * pl.reciprocal(
                    dd + column_term[here, h * 128 : (h + 1) * 128], approx=True
                )
                cover[here, pl.ds(base + h * 128, 128)] = c.astype(jnp.bfloat16)
        total[...] += lax.dot_general(
            cover[:, pl.ds(base, columns)],
            estimate[:, pl.ds(base, columns)],
            NT,
            preferred_element_type=jnp.float32,
        )
        return carry

    lax.fori_loop(0, rows, row, 0)
    for s in range(GROUP):
        slot = step * GROUP + s
        value = jnp.transpose(total[s * antennas : (s + 1) * antennas, :])
        block = meta[slot]
        partial[block] = jnp.where(slot < meta[slots], partial[block] + value, partial[block])


def fill_weights(meta, settings, shares, weights):
    slots, antennas, maps = meta.shape[0] - 3, settings.shape[2], shares.shape[1]

    def pieces(x):
        high = x.astype(jnp.bfloat16)
        return high, x - high.astype(jnp.float32)

    first = lax.broadcasted_iota(jnp.int32, (16, antennas), 0)
    for s in range(slots):
        here = slice(s * antennas, (s + 1) * antennas)
        block = meta[s]
        live = s < meta[slots]
        high, rest = pieces(jnp.where(live, shares[block], 0.0))
        weights[0:maps, here] = high
        weights[maps : 2 * maps, here] = rest.astype(jnp.bfloat16)
        gain = jnp.where(live, jnp.broadcast_to(settings[block][3:4, :], (16, antennas)), 0.0)
        g0, rest = pieces(gain)
        g1, rest = pieces(rest)
        f0, f1, f2 = g0.astype(jnp.float32), g1.astype(jnp.float32), rest
        rows = jnp.where(first == 0, f0, jnp.where(first == 1, f1, jnp.where(first == 2, f2, 0.0)))
        weights[2 * maps : 2 * maps + 16, here] = rows.astype(jnp.bfloat16)


def updated(weights, cover, estimate):
    maps = estimate.shape[0]
    sums = jnp.dot(weights[...], cover[...], preferred_element_type=jnp.float32)
    sens = jnp.sum(sums[2 * maps :, :], axis=0, keepdims=True)
    return estimate[...] * (sums[:maps, :] + sums[maps : 2 * maps, :]) / sens


def middle_kernel(meta, settings, shares, cover, estimate, new, partial, weights, total):
    slots, antennas = meta.shape[0] - 3, settings.shape[2]
    step = pl.program_id(0)

    @pl.when(step == 0)
    def _():
        partial[...] = jnp.zeros_like(partial)
        total[...] = jnp.zeros_like(total)
        fill_weights(meta, settings, shares, weights)

    value = updated(weights, cover, estimate)
    new[...] = value
    narrow = value.astype(jnp.bfloat16)
    depth = GROUP * antennas
    for g in range(slots // GROUP):
        here = slice(g * depth, (g + 1) * depth)
        total[here, :] += lax.dot_general(
            cover[here, :], narrow, NT, preferred_element_type=jnp.float32
        )

    @pl.when(step == pl.num_programs(0) - 1)
    def _():
        for s in range(slots):
            value = jnp.transpose(total[s * antennas : (s + 1) * antennas, :])
            block = meta[s]
            partial[block] = jnp.where(s < meta[slots], partial[block] + value, partial[block])


def last_kernel(meta, settings, shares, cover, estimate, new, weights):
    @pl.when(pl.program_id(0) == 0)
    def _():
        fill_weights(meta, settings, shares, weights)

    new[...] = updated(weights, cover, estimate)


def whole(shape):
    return pl.BlockSpec(shape, lambda i, meta: (0,) * len(shape))


def shards(initial_estimate0, clutter, counts, antenna_settings, tile_block_list, tile_block_count):
    maps, rows, columns = initial_estimate0.shape
    n_pixels = rows * columns
    antennas = antenna_settings.shape[2]
    slots = tile_block_list.shape[2]
    n_blocks = lax.axis_size(("row", "col")) * counts.shape[0]
    depth = GROUP * antennas
    meta = jnp.concatenate(
        [
            tile_block_list.reshape(slots),
            tile_block_count.reshape(1),
            (lax.axis_index("row") * rows).astype(jnp.int32).reshape(1),
            (lax.axis_index("col") * columns).astype(jnp.int32).reshape(1),
        ]
    )
    estimate = initial_estimate0.reshape(maps, n_pixels)
    settings = lax.all_gather(
        jnp.pad(antenna_settings, ((0, 0), (0, 3), (0, 0))), ("row", "col"), axis=0, tiled=True
    )
    params = pltpu.CompilerParams(vmem_limit_bytes=VMEM, dimension_semantics=("arbitrary",))
    partial_shape = jax.ShapeDtypeStruct((n_blocks, maps, antennas), jnp.float32)
    cover, partial = pl.pallas_call(
        cover_kernel,
        out_shape=(
            jax.ShapeDtypeStruct((slots * antennas, n_pixels), jnp.bfloat16),
            partial_shape,
        ),
        grid_spec=pltpu.PrefetchScalarGridSpec(
            num_scalar_prefetch=1,
            grid=(slots // GROUP,),
            in_specs=[
                whole(settings.shape),
                whole((rows, 1, columns)),
                whole((maps, n_pixels)),
            ],
            out_specs=[
                pl.BlockSpec((depth, n_pixels), lambda i, meta: (i, 0)),
                whole(partial_shape.shape),
            ],
            scratch_shapes=[
                pltpu.VMEM((depth, columns), jnp.float32),
                pltpu.VMEM((depth, 128), jnp.float32),
                pltpu.VMEM((depth, 128), jnp.float32),
                pltpu.VMEM((depth, 128), jnp.float32),
                pltpu.VMEM((depth, maps), jnp.float32),
            ],
        ),
        compiler_params=params,
        name="cover_first",
    )(meta, settings, clutter.reshape(rows, 1, columns), estimate.astype(jnp.bfloat16))

    def share(partial):
        projected = lax.psum_scatter(partial, ("row", "col"), scatter_dimension=0, tiled=True)
        return lax.all_gather(
            counts.astype(jnp.float32) / projected, ("row", "col"), axis=0, tiled=True
        )

    pixel_spec = pl.BlockSpec((maps, CHUNK), lambda i, meta: (0, i))
    estimate_shape = jax.ShapeDtypeStruct((maps, n_pixels), jnp.float32)
    in_specs = [
        whole(settings.shape),
        whole(partial_shape.shape),
        pl.BlockSpec((slots * antennas, CHUNK), lambda i, meta: (0, i)),
        pixel_spec,
    ]
    weights = pltpu.VMEM((2 * maps + 16, slots * antennas), jnp.bfloat16)
    for sweep in range(ITERS - 1):
        estimate, partial = pl.pallas_call(
            middle_kernel,
            out_shape=(estimate_shape, partial_shape),
            grid_spec=pltpu.PrefetchScalarGridSpec(
                num_scalar_prefetch=1,
                grid=(n_pixels // CHUNK,),
                in_specs=in_specs,
                out_specs=[pixel_spec, whole(partial_shape.shape)],
                scratch_shapes=[weights, pltpu.VMEM((slots * antennas, maps), jnp.float32)],
            ),
            compiler_params=params,
            name="update_project",
        )(meta, settings, share(partial), cover, estimate)
    estimate = pl.pallas_call(
        last_kernel,
        out_shape=estimate_shape,
        grid_spec=pltpu.PrefetchScalarGridSpec(
            num_scalar_prefetch=1,
            grid=(n_pixels // CHUNK,),
            in_specs=in_specs,
            out_specs=pixel_spec,
            scratch_shapes=[weights],
        ),
        compiler_params=params,
        name="update_last",
    )(meta, settings, share(partial), cover, estimate)
    return estimate.reshape(maps, rows, columns)


def solution(mesh):
    in_specs = (
        P(None, "row", "col"),
        P("row", "col"),
        P(("row", "col"), None, None),
        P(("row", "col"), None, None),
        P("row", "col", None),
        P("row", "col"),
    )
    out_specs = P(None, "row", "col")
    return jax.shard_map(shards, mesh=mesh, in_specs=in_specs, out_specs=out_specs, check_vma=False)
```

profile of v0, /device:TPU:0, one launch (start us, length us, event | category | flops | bytes accessed | tf_op | source)
XLA Modules:
  0.0 463.7 jit_solution(93055866004207228)
XLA Ops:
  6.5 0.0 reduce-scatter.3.cloned.1.call-start
  7.2 0.7 copy.8
  7.9 0.7 reshape.25.clutter
  8.6 43.6 %all_gather.9.settings = f32[32,8,128]{2,1,0:T(8,128)S(1)} all-gather(f32[1,8,128]{2,1,0:T(8,128)S(1)} %pad.4), channel_id=1, replica_groups=mesh['row'=8,'col'=4] {'row','col'}, dimensions={0}, use_global_device_ids=true | all-gather | bytes 135168 | tf_op jit(solution)/shard_map/all_gather | solution.py:160
  52.2 2.5 copy.9
  54.7 0.0 copy-start.2
  54.7 0.0 copy-start.4
  54.7 0.1 convert_element_type.10.estimate
  54.8 0.0 copy-start.3
  54.8 0.6 copy-done.4
  55.4 0.1 pad_add_fusion.meta
  55.5 53.7 %cover_first.1 = (bf16[4096,4096]{1,0:T(8,128)(2,1)}, f32[32,96,128]{2,1,0:T(8,128)}) custom-call(s32[35]{0:T(128)S(1)} %pad_add_fusion.meta, f32[32,8,128]{2,1,0:T(8,128)S(1)} %all_gather.9.settings, f32[16,1,256]{2,1,0:T(1,128)S(1)} %reshape.25.clutter, bf16[96,4096]{1,0:T(8,128)(2,1)S(1)} %convert_element_type.10.estimate), custom_call_target="tpu_custom_call" | custom-call | tf_op jit(solution)/shard_map/cover_first/pallas_call | solution.py:165
  109.1 0.0 copy-done.2
  109.1 0.0 reduce-scatter.3.cloned.1.call-update
  109.2 0.0 all-gather.3.cloned.1.call-start
  109.2 93.2 %reduce-scatter.3.cloned.1.call-done = f32[1,96,128]{2,1,0:T(8,128)} async-done(((f32[32,96,128]{2,1,0:T(8,128)}), f32[1,96,128]{2,1,0:T(8,128)}) %reduce-scatter.3.cloned.1.call-update) | async-done | bytes 49168 | tf_op jit(solution)/shard_map/reduce_scatter | solution.py:196
  202.4 0.0 copy-done.3
  202.4 1.4 convert_divide_fusion.1
  203.9 0.0 all-gather.3.cloned.1.call-update
  203.9 0.0 reduce-scatter.5.cloned.1.call-start
  203.9 55.5 %all-gather.3.cloned.1.call-done.shares = f32[32,96,128]{2,1,0:T(8,128)} async-done(((f32[1,96,128]{2,1,0:T(8,128)}), f32[32,96,128]{2,1,0:T(8,128)}) %all-gather.3.cloned.1.call-update) | async-done | bytes 1572880 | tf_op jit(solution)/shard_map/all_gather | solution.py:197
  259.4 24.6 %update_project.1 = (f32[96,4096]{1,0:T(8,128)S(1)}, f32[32,96,128]{2,1,0:T(8,128)}) custom-call(s32[35]{0:T(128)S(1)} %pad_add_fusion.meta, f32[32,8,128]{2,1,0:T(8,128)S(1)} %all_gather.9.settings, f32[32,96,128]{2,1,0:T(8,128)} %all-gather.3.cloned.1.call-done.shares, bf16[4096,4096]{1,0:T(8,128)(2,1)} %get-tuple-element.10.cover, f32[96,4096]{1,0:T(8,128)} %bitcast.11), custom_call_target="tpu_custom_call" | custom-call | tf_op jit(solution)/shard_map/update_project/pallas_call | solution.py:211
  284.0 1.1 copy-done
  285.1 0.0 reduce-scatter.5.cloned.1.call-update
  285.1 0.0 all-gather.5.cloned.1.call-start
  285.2 96.0 %reduce-scatter.5.cloned.1.call-done = f32[1,96,128]{2,1,0:T(8,128)} async-done(((f32[32,96,128]{2,1,0:T(8,128)}), f32[1,96,128]{2,1,0:T(8,128)}) %reduce-scatter.5.cloned.1.call-update) | async-done | bytes 49168 | tf_op jit(solution)/shard_map/reduce_scatter | solution.py:196
  381.2 1.4 convert_divide_fusion
  382.7 0.0 all-gather.5.cloned.1.call-update
  382.7 55.4 %all-gather.5.cloned.1.call-done.shares = f32[32,96,128]{2,1,0:T(8,128)} async-done(((f32[1,96,128]{2,1,0:T(8,128)}), f32[32,96,128]{2,1,0:T(8,128)}) %all-gather.5.cloned.1.call-update) | async-done | bytes 1572880 | tf_op jit(solution)/shard_map/all_gather | solution.py:197
  438.1 1.4 copy-done.1
  439.5 16.1 %update_last.1 = f32[96,4096]{1,0:T(8,128)S(1)} custom-call(s32[35]{0:T(128)S(1)} %pad_add_fusion.meta, f32[32,8,128]{2,1,0:T(8,128)S(1)} %all_gather.9.settings, f32[32,96,128]{2,1,0:T(8,128)S(1)} %copy-done.1, bf16[4096,4096]{1,0:T(8,128)(2,1)} %get-tuple-element.10.cover, f32[96,4096]{1,0:T(8,128)} %copy-done), custom_call_target="tpu_custom_call" | custom-call | tf_op jit(solution)/shard_map/update_last/pallas_call | solution.py:224
  455.6 1.6 copy.10
  (3 shorter events, 0.0 us)
Async XLA Ops:
  6.5 195.9 %reduce-scatter.3.cloned.1.call-start = ((), (), s32[]{:S(2)}) async-start(), calls=%async_computation.2 | async-start | bytes 1622016 | tf_op jit(solution)/shard_map/reduce_scatter | solution.py:196
  54.7 54.4 %copy-start.2 = (f32[12,8,16,256]{3,1,2,0:T(8,128)}, f32[12,8,16,256]{3,1,2,0:T(8,128)S(1)}, u32[]{:S(2)}) copy-start(f32[12,8,16,256]{3,1,2,0:T(8,128)S(1)} %copy.9) | copy-start | bytes 4718596
  54.7 0.7 copy-start.4
  54.8 147.6 %copy-start.3 = (s32[1,96,128]{2,1,0:T(8,128)S(1)}, s32[1,96,128]{2,1,0:T(8,128)}, u32[]{:S(2)}) copy-start(s32[1,96,128]{2,1,0:T(8,128)} %param.8) | copy-start | bytes 147460
  109.2 150.3 %all-gather.3.cloned.1.call-start = ((), (), s32[]{:S(2)}) async-start(), calls=%async_computation.3 | async-start | bytes 1622016 | tf_op jit(solution)/shard_map/all_gather | solution.py:197
  203.9 177.3 %reduce-scatter.5.cloned.1.call-start = ((), (), s32[]{:S(2)}) async-start(), calls=%async_computation.4 | async-start | bytes 1622016 | tf_op jit(solution)/shard_map/reduce_scatter | solution.py:196
  284.0 1.1 copy-start
  285.1 152.9 %all-gather.5.cloned.1.call-start = ((), (), s32[]{:S(2)}) async-start(), calls=%async_computation.5 | async-start | bytes 1622016 | tf_op jit(solution)/shard_map/all_gather | solution.py:197
  438.0 1.4 copy-start.1
Sparse Core Ops, SparseCore 0:
  109.3 93.1 reduce-scatter.2
  205.3 54.0 all-gather.2
  285.3 95.9 reduce-scatter.4
  384.0 54.0 all-gather.4
where the time goes:
time: 464 us
  waiting for transfers between devices  300 us (65%)
  Pallas kernels  94.3 us (20%)
  blocking collectives  43.6 us (9%)
  between operations  13.8 us (3%)
  local copies, waits for them, and re-layouts  8.67 us (2%)
    reduce_scatter x2, waiting for transfers between devices, share(): lax.psum_scatter(partial, ('row', 'col'), scatter_dimension=0, tiled=True)  189 us
    all_gather x2, waiting for transfers between devices, share(): lax.all_gather(counts.astype(jnp.float32) / projected, ('row', 'col'), ax...  111 us
    pallas_call x1, Pallas kernels, shards(): pl.pallas_call(cover_kernel, out_shape=(jax.ShapeDtypeStruct((slots * ant...  53.7 us
    all_gather x1, blocking collectives, shards(): lax.all_gather(jnp.pad(antenna_settings, ((0, 0), (0, 3), (0, 0))), ('row...  43.6 us
    pallas_call x1, Pallas kernels, shards(): pl.pallas_call(middle_kernel, out_shape=(estimate_shape, partial_shape),...  24.6 us
    pallas_call x1, Pallas kernels, shards(): pl.pallas_call(last_kernel, out_shape=estimate_shape, grid_spec=pltpu.Pre...  16.1 us
  transfers between devices with their start and end apart: 4, of which 4 were waited for; matrix products, arithmetic and copies ran while one was open for 0% of the time, Pallas kernels for 0%

commit v1 on v0

--- a/solution.py
+++ b/solution.py
@@ -1,3 +1,5 @@
+import functools
+
 import jax
 import jax.numpy as jnp
 from jax import lax
@@ -11,6 +13,147 @@
 LOG2E = 1.4426950408889634
 NT = (((1,), (1,)), ((), ()))
 VMEM = 50 << 20
+MESH = pl.DeviceIdType.MESH
+PARTS = 3
+
+
+def place(n_row, n_col):
+    row, col = lax.axis_index("row"), lax.axis_index("col")
+    rh, rl, ch, cl = row // 2, row % 2, col // 2, col % 2
+    far_col, far_row = n_col // 2, n_row // 2
+    ch_peers = [(ch + k) % far_col for k in range(1, far_col)]
+    rh_peers = [(rh + k) % far_row for k in range(1, far_row)]
+    partners = [
+        [(row, col + 1 - 2 * cl)],
+        [(row, p * 2 + cl) for p in ch_peers],
+        [(row + 1 - 2 * rl, col)],
+        [(p * 2 + rl, col) for p in rh_peers],
+    ]
+    return (rh, rl, ch, cl), ch_peers, rh_peers, partners
+
+
+def greet(partners):
+    barrier = pltpu.get_barrier_semaphore()
+    everyone = [d for step in partners for d in step]
+    for device in everyone:
+        pl.semaphore_signal(barrier, inc=1, device_id=device, device_id_type=MESH)
+    pl.semaphore_wait(barrier, len(everyone))
+
+
+def launch(pairs, partners, send, recv, first):
+    copies = []
+    for k, ((source, target), device) in enumerate(zip(pairs, partners)):
+        copy = pltpu.make_async_remote_copy(
+            src_ref=source,
+            dst_ref=target,
+            send_sem=send.at[first + k],
+            recv_sem=recv.at[first + k],
+            device_id=device,
+            device_id_type=MESH,
+        )
+        copy.start()
+        copies.append(copy)
+    return copies
+
+
+def spread(out, digits, partners, cuts, send, recv, first):
+    rh, rl, ch, cl = digits
+    started = []
+    before = None
+    for step in (3, 2, 1, 0):
+        current = []
+        for q, cut in enumerate(cuts):
+            if before is not None:
+                for copy in before[q]:
+                    copy.wait_recv()
+            view = (
+                out.at[:, :, :, cl, cut],
+                out.at[:, :, ch, cl, cut],
+                out.at[:, rl, ch, cl, cut],
+                out.at[rh, rl, ch, cl, cut],
+            )[step]
+            pairs = [(view, view)] * len(partners[step])
+            current.append(launch(pairs, partners[step], send, recv, first))
+            first += len(pairs)
+            started += current[-1]
+        before = current
+    for group in before:
+        for copy in group:
+            copy.wait_recv()
+    for copy in started:
+        copy.wait_send()
+
+
+def gather_kernel(n_row, n_col, mine, out, send, recv):
+    digits, _, _, partners = place(n_row, n_col)
+    rh, rl, ch, cl = digits
+    greet(partners)
+    out[rh, rl, ch, cl] = mine[0]
+    spread(out, digits, partners, [slice(0, mine.shape[1])], send, recv, 0)
+
+
+def share_kernel(
+    n_row, n_col, partial, counts, out, in0, in1, in2, in3, sum0, sum1, sum2, send, recv
+):
+    digits, ch_peers, rh_peers, partners = place(n_row, n_col)
+    rh, rl, ch, cl = digits
+    maps = counts.shape[1]
+    piece = maps // PARTS
+    cuts = [slice(q * piece, (q + 1) * piece) for q in range(PARTS)]
+    greet(partners)
+    first, started, before = 0, [], None
+    for step in range(5):
+        current = []
+        for q, cut in enumerate(cuts):
+            if before is not None:
+                for copy in before[q]:
+                    copy.wait_recv()
+            if step == 0:
+                pairs = [(partial.at[:, :, :, 1 - cl, cut], in0.at[:, :, :, cut])]
+            elif step == 1:
+                sum0[:, :, :, cut] = partial[:, :, :, cl, cut] + in0[:, :, :, cut]
+                pairs = [
+                    (sum0.at[:, :, p, cut], in1.at[k, :, :, cut]) for k, p in enumerate(ch_peers)
+                ]
+            elif step == 2:
+                value = sum0[:, :, ch, cut]
+                for k in range(len(ch_peers)):
+                    value = value + in1[k, :, :, cut]
+                sum1[:, :, cut] = value
+                pairs = [(sum1.at[:, 1 - rl, cut], in2.at[:, cut])]
+            elif step == 3:
+                sum2[:, cut] = sum1[:, rl, cut] + in2[:, cut]
+                pairs = [(sum2.at[p, cut], in3.at[k, cut]) for k, p in enumerate(rh_peers)]
+            else:
+                value = sum2[rh, cut]
+                for k in range(len(rh_peers)):
+                    value = value + in3[k, cut]
+                out[rh, rl, ch, cl, cut] = counts[0, cut].astype(jnp.float32) / value
+                continue
+            current.append(launch(pairs, partners[step], send, recv, first))
+            first += len(pairs)
+            started += current[-1]
+        before = current
+    spread(out, digits, partners, cuts, send, recv, first)
+    for copy in started:
+        copy.wait_send()
+
+
+def exchange(kernel, n_row, n_col, operands, block, scratch, copies, number, name):
+    grid = (n_row // 2, 2, n_col // 2, 2)
+    out = pl.pallas_call(
+        functools.partial(kernel, n_row, n_col),
+        out_shape=jax.ShapeDtypeStruct(grid + block, jnp.float32),
+        in_specs=[pl.BlockSpec(memory_space=pltpu.VMEM)] * len(operands),
+        out_specs=pl.BlockSpec(memory_space=pltpu.VMEM),
+        scratch_shapes=[pltpu.VMEM(shape + block, jnp.float32) for shape in scratch]
+        + [pltpu.SemaphoreType.DMA((copies,)), pltpu.SemaphoreType.DMA((copies,))],
+        compiler_params=pltpu.CompilerParams(
+            collective_id=number, has_side_effects=True, vmem_limit_bytes=VMEM
+        ),
+        name=name,
+    )(*operands)
+    return out.reshape((n_row * n_col,) + block)
 
 
 def cover_kernel(
@@ -157,8 +300,18 @@
         ]
     )
     estimate = initial_estimate0.reshape(maps, n_pixels)
-    settings = lax.all_gather(
-        jnp.pad(antenna_settings, ((0, 0), (0, 3), (0, 0))), ("row", "col"), axis=0, tiled=True
+    n_row, n_col = lax.axis_size("row"), lax.axis_size("col")
+    far_row, far_col = n_row // 2, n_col // 2
+    settings = exchange(
+        gather_kernel,
+        n_row,
+        n_col,
+        (jnp.pad(antenna_settings, ((0, 0), (0, 3), (0, 0))),),
+        (8, antennas),
+        [],
+        far_row + far_col,
+        1,
+        "gather_settings",
     )
     params = pltpu.CompilerParams(vmem_limit_bytes=VMEM, dimension_semantics=("arbitrary",))
     partial_shape = jax.ShapeDtypeStruct((n_blocks, maps, antennas), jnp.float32)
@@ -193,9 +346,24 @@
     )(meta, settings, clutter.reshape(rows, 1, columns), estimate.astype(jnp.bfloat16))
 
     def share(partial):
-        projected = lax.psum_scatter(partial, ("row", "col"), scatter_dimension=0, tiled=True)
-        return lax.all_gather(
-            counts.astype(jnp.float32) / projected, ("row", "col"), axis=0, tiled=True
+        return exchange(
+            share_kernel,
+            n_row,
+            n_col,
+            (partial.reshape(far_row, 2, far_col, 2, maps, antennas), counts),
+            (maps, antennas),
+            [
+                (far_row, 2, far_col),
+                (far_col - 1, far_row, 2),
+                (far_row,),
+                (far_row - 1,),
+                (far_row, 2, far_col),
+                (far_row, 2),
+                (far_row,),
+            ],
+            2 * PARTS * (far_row + far_col),
+            2,
+            "share_ratios",
         )
 
     pixel_spec = pl.BlockSpec((maps, CHUNK), lambda i, meta: (0, i))

time: 464 us -> 192 us (0.41)
  waiting for transfers between devices: 300 us -> 0 us
  Pallas kernels: 94.3 us -> 182 us
  blocking collectives: 43.6 us -> 0 us
  between operations: 13.8 us -> 0.74 us
    reduce_scatter x2 -> x0, waiting for transfers between devices: 189 us -> none  [share(): lax.psum_scatter(partial, ('row', 'col'), scatter_dimension=0, tiled=True)]
    all_gather x2 -> x0, waiting for transfers between devices: 111 us -> none  [share(): lax.all_gather(counts.astype(jnp.float32) / projected, ('row', 'col'), ax...]
    pallas_call x0 -> x3, Pallas kernels: none -> 89.6 us  [exchange(): pl.pallas_call(functools.partial(kernel, n_row, n_col), out_shape=jax.Sha...]
    all_gather x1 -> x0, blocking collectives: 43.6 us -> none  [shards(): lax.all_gather(jnp.pad(antenna_settings, ((0, 0), (0, 3), (0, 0))), ('row...]
  transfers between devices with their start and end apart: 4 -> 0, of which waited for: 4 -> 0; matrix products, arithmetic and copies ran while one was open for 0% -> 0% of each run, Pallas kernels for 0% -> 0%
where the time goes in v1:
time: 192 us
  Pallas kernels  182 us (95%)
  local copies, waits for them, and re-layouts  7.84 us (4%)
    pallas_call x3, Pallas kernels, exchange(): pl.pallas_call(functools.partial(kernel, n_row, n_col), out_shape=jax.Sha...  89.6 us
    pallas_call x1, Pallas kernels, shards(): pl.pallas_call(cover_kernel, out_shape=(jax.ShapeDtypeStruct((slots * ant...  53.3 us
    pallas_call x1, Pallas kernels, shards(): pl.pallas_call(middle_kernel, out_shape=(estimate_shape, partial_shape),...  23.4 us
    pallas_call x1, Pallas kernels, shards(): pl.pallas_call(last_kernel, out_shape=estimate_shape, grid_spec=pltpu.Pre...  16.1 us
    unnamed x11, local copies, waits for them, and re-layouts  7.1 us

profile of v1, /device:TPU:0, one launch (start us, length us, event | category | flops | bytes accessed | tf_op | source)
XLA Modules:
  0.0 191.8 jit_solution(14591150905472860595)
XLA Ops:
  0.7 0.7 pad_add_fusion.meta
  1.4 0.7 copy.7
  2.1 0.7 reshape.41.clutter
  2.8 14.9 %gather_settings.1 = f32[4,2,2,2,8,128]{5,4,3,2,1,0:T(8,128)S(1)} custom-call(f32[1,8,128]{2,1,0:T(8,128)S(1)} %pad.4.mine), custom_call_target="tpu_custom_call" | custom-call | tf_op jit(solution)/shard_map/gather_settings/pallas_call | solution.py:144
  17.8 2.5 %copy.8 = f32[12,8,16,256]{3,1,2,0:T(8,128)S(1)} copy(f32[12,8,16,256]{3,2,1,0:T(8,128)} %bitcast.24) | data formatting | bytes 3145728
  20.3 0.0 copy-start.3
  20.3 0.0 copy-start.2
  20.3 0.1 convert_element_type.5.estimate
  20.4 53.3 %cover_first.1 = (bf16[4096,4096]{1,0:T(8,128)(2,1)}, f32[32,96,128]{2,1,0:T(8,128)S(1)}) custom-call(s32[35]{0:T(128)S(1)} %pad_add_fusion.meta, f32[32,8,128]{2,1,0:T(8,128)S(1)} %bitcast.17, f32[16,1,256]{2,1,0:T(1,128)S(1)} %reshape.41.clutter, bf16[96,4096]{1,0:T(8,128)(2,1)S(1)} %convert_element_type.5.estimate), custom_call_target="tpu_custom_call" | custom-call | tf_op jit(solution)/shard_map/cover_first/pallas_call | solution.py:318
  73.7 0.0 copy-done.3
  73.7 0.0 copy-done.2
  73.7 38.4 %share_ratios.2 = f32[4,2,2,2,96,128]{5,4,3,2,1,0:T(8,128)S(1)} custom-call(f32[4,2,2,2,96,128]{5,4,3,2,1,0:T(8,128)S(1)} %bitcast.20, s32[1,96,128]{2,1,0:T(8,128)S(1)} %copy-done.2), custom_call_target="tpu_custom_call" | custom-call | tf_op jit(solution)/shard_map/share_ratios/pallas_call | solution.py:144
  112.1 0.0 copy-start
  112.1 1.1 copy-done
  113.2 23.4 %update_project.1 = (f32[96,4096]{1,0:T(8,128)S(1)}, f32[32,96,128]{2,1,0:T(8,128)S(1)}) custom-call(s32[35]{0:T(128)S(1)} %pad_add_fusion.meta, f32[32,8,128]{2,1,0:T(8,128)S(1)} %bitcast.18, f32[32,96,128]{2,1,0:T(8,128)} %bitcast.16, bf16[4096,4096]{1,0:T(8,128)(2,1)} %get-tuple-element.10.cover, f32[96,4096]{1,0:T(8,128)} %bitcast.23), custom_call_target="tpu_custom_call" | custom-call | tf_op jit(solution)/shard_map/update_project/pallas_call | solution.py:379
  136.6 0.0 copy-start.1
  136.6 1.1 copy-done.1
  137.8 36.3 %share_ratios.3 = f32[4,2,2,2,96,128]{5,4,3,2,1,0:T(8,128)S(1)} custom-call(f32[4,2,2,2,96,128]{5,4,3,2,1,0:T(8,128)S(1)} %bitcast.21, s32[1,96,128]{2,1,0:T(8,128)S(1)} %copy-done.2), custom_call_target="tpu_custom_call" | custom-call | tf_op jit(solution)/shard_map/share_ratios/pallas_call | solution.py:144
  174.1 16.1 %update_last.1 = f32[96,4096]{1,0:T(8,128)S(1)} custom-call(s32[35]{0:T(128)S(1)} %pad_add_fusion.meta, f32[32,8,128]{2,1,0:T(8,128)S(1)} %bitcast.19, f32[32,96,128]{2,1,0:T(8,128)S(1)} %bitcast.14, bf16[4096,4096]{1,0:T(8,128)(2,1)} %get-tuple-element.10.cover, f32[96,4096]{1,0:T(8,128)} %copy-done.1), custom_call_target="tpu_custom_call" | custom-call | tf_op jit(solution)/shard_map/update_last/pallas_call | solution.py:392
  190.2 1.6 copy.9
  (1 shorter events, 0.0 us)
Async XLA Ops:
  20.3 53.4 %copy-start.3 = (f32[12,8,16,256]{3,1,2,0:T(8,128)}, f32[12,8,16,256]{3,1,2,0:T(8,128)S(1)}, u32[]{:S(2)}) copy-start(f32[12,8,16,256]{3,1,2,0:T(8,128)S(1)} %copy.8) | copy-start | bytes 4718596
  20.3 53.4 %copy-start.2 = (s32[1,96,128]{2,1,0:T(8,128)S(1)}, s32[1,96,128]{2,1,0:T(8,128)}, u32[]{:S(2)}) copy-start(s32[1,96,128]{2,1,0:T(8,128)} %counts.3) | copy-start | bytes 147460
  112.1 1.1 copy-start
  136.6 1.1 copy-start.1

commit v2 on v1

--- a/solution.py
+++ b/solution.py
@@ -157,7 +157,8 @@
 
 
 def cover_kernel(
-    meta, settings, clutter, estimate, cover, partial, column_term, slope, shift, inverse, total
+    meta, settings, clutter, estimate, cover, partial, column_term, slope, shift, inverse, total,
+    turned,
 ):
     slots, rows, columns = meta.shape[0] - 3, clutter.shape[0], clutter.shape[2]
     antennas = settings.shape[2]
@@ -167,6 +168,9 @@
     @pl.when(step == 0)
     def _():
         partial[...] = jnp.zeros_like(partial)
+        for i in range(rows):
+            here = slice(i * columns, (i + 1) * columns)
+            turned[here, :] = jnp.transpose(estimate[:, here]).astype(jnp.bfloat16)
 
     row_start = meta[slots + 1].astype(jnp.float32) + 0.5
     column_start = meta[slots + 2].astype(jnp.float32) + 0.5
@@ -187,8 +191,10 @@
     def row(i, carry):
         base = pl.multiple_of(i * columns, columns)
         offset = i.astype(jnp.float32)
+        blocks = []
         for s in range(GROUP):
             here = slice(s * antennas, (s + 1) * antennas)
+            halves = []
             d = shift[here, :] + offset * inverse[here, :]
             dd = d * d
             k = slope[here, :]
@@ -197,16 +203,17 @@
                 c = jnp.exp2(k * loss) * pl.reciprocal(
                     dd + column_term[here, h * 128 : (h + 1) * 128], approx=True
                 )
-                cover[here, pl.ds(base + h * 128, 128)] = c.astype(jnp.bfloat16)
-        total[...] += lax.dot_general(
-            cover[:, pl.ds(base, columns)],
-            estimate[:, pl.ds(base, columns)],
-            NT,
+                halves.append(c.astype(jnp.bfloat16))
+            blocks.append(jnp.concatenate(halves, axis=1))
+            cover[here, pl.ds(base, columns)] = blocks[-1]
+        total[...] += jnp.dot(
+            jnp.concatenate(blocks, axis=0),
+            turned[pl.ds(base, columns), :],
             preferred_element_type=jnp.float32,
         )
         return carry
 
-    lax.fori_loop(0, rows, row, 0)
+    lax.fori_loop(0, rows, row, 0, unroll=2)
     for s in range(GROUP):
         slot = step * GROUP + s
         value = jnp.transpose(total[s * antennas : (s + 1) * antennas, :])
@@ -339,11 +346,12 @@
                 pltpu.VMEM((depth, 128), jnp.float32),
                 pltpu.VMEM((depth, 128), jnp.float32),
                 pltpu.VMEM((depth, maps), jnp.float32),
+                pltpu.VMEM((n_pixels, maps), jnp.bfloat16),
             ],
         ),
         compiler_params=params,
         name="cover_first",
-    )(meta, settings, clutter.reshape(rows, 1, columns), estimate.astype(jnp.bfloat16))
+    )(meta, settings, clutter.reshape(rows, 1, columns), estimate)
 
     def share(partial):
         return exchange(

time: 192 us -> 177 us (0.922)
  Pallas kernels: 182 us -> 167 us
    pallas_call x1, Pallas kernels: 53.3 us -> 38.5 us  [shards(): pl.pallas_call(cover_kernel, out_shape=(jax.ShapeDtypeStruct((slots * ant...]
where the time goes in v2:
time: 177 us
  Pallas kernels  167 us (94%)
  local copies, waits for them, and re-layouts  7.84 us (4%)
    pallas_call x3, Pallas kernels, exchange(): pl.pallas_call(functools.partial(kernel, n_row, n_col), out_shape=jax.Sha...  89.5 us
    pallas_call x1, Pallas kernels, shards(): pl.pallas_call(cover_kernel, out_shape=(jax.ShapeDtypeStruct((slots * ant...  38.5 us
    pallas_call x1, Pallas kernels, shards(): pl.pallas_call(middle_kernel, out_shape=(estimate_shape, partial_shape),...  23.4 us
    pallas_call x1, Pallas kernels, shards(): pl.pallas_call(last_kernel, out_shape=estimate_shape, grid_spec=pltpu.Pre...  16.1 us
    unnamed x11, local copies, waits for them, and re-layouts  7.1 us

profile of v2, /device:TPU:0, one launch (start us, length us, event | category | flops | bytes accessed | tf_op | source)
XLA Modules:
  0.0 176.8 jit_solution(14790001204798132008)
XLA Ops:
  0.7 0.7 pad_add_fusion.meta
  1.4 0.7 copy.7
  2.1 0.7 reshape.41.clutter
  2.8 14.9 %gather_settings.1 = f32[4,2,2,2,8,128]{5,4,3,2,1,0:T(8,128)S(1)} custom-call(f32[1,8,128]{2,1,0:T(8,128)S(1)} %pad.4.mine), custom_call_target="tpu_custom_call" | custom-call | tf_op jit(solution)/shard_map/gather_settings/pallas_call | solution.py:144
  17.8 2.5 %copy.8 = f32[12,8,16,256]{3,1,2,0:T(8,128)S(1)} copy(f32[12,8,16,256]{3,2,1,0:T(8,128)} %bitcast.24) | data formatting | bytes 3145728
  20.3 0.0 copy-start
  20.3 0.0 copy-start.3
  20.3 38.5 %cover_first.1 = (bf16[4096,4096]{1,0:T(8,128)(2,1)}, f32[32,96,128]{2,1,0:T(8,128)S(1)}) custom-call(s32[35]{0:T(128)S(1)} %pad_add_fusion.meta, f32[32,8,128]{2,1,0:T(8,128)S(1)} %bitcast.19, f32[16,1,256]{2,1,0:T(1,128)S(1)} %reshape.41.clutter, f32[96,4096]{1,0:T(8,128)S(1)} %bitcast.14), custom_call_target="tpu_custom_call" | custom-call | tf_op jit(solution)/shard_map/cover_first/pallas_call | solution.py:325
  58.8 0.0 copy-done.3
  58.8 38.4 %share_ratios.2 = f32[4,2,2,2,96,128]{5,4,3,2,1,0:T(8,128)S(1)} custom-call(f32[4,2,2,2,96,128]{5,4,3,2,1,0:T(8,128)S(1)} %bitcast.23, s32[1,96,128]{2,1,0:T(8,128)S(1)} %copy-done.3), custom_call_target="tpu_custom_call" | custom-call | tf_op jit(solution)/shard_map/share_ratios/pallas_call | solution.py:144
  97.2 0.0 copy-done
  97.2 0.0 copy-start.1
  97.2 1.1 copy-done.1
  98.3 23.4 %update_project.1 = (f32[96,4096]{1,0:T(8,128)S(1)}, f32[32,96,128]{2,1,0:T(8,128)S(1)}) custom-call(s32[35]{0:T(128)S(1)} %pad_add_fusion.meta, f32[32,8,128]{2,1,0:T(8,128)S(1)} %bitcast.20, f32[32,96,128]{2,1,0:T(8,128)} %bitcast.18, bf16[4096,4096]{1,0:T(8,128)(2,1)} %get-tuple-element.10.cover, f32[96,4096]{1,0:T(8,128)} %bitcast.15), custom_call_target="tpu_custom_call" | custom-call | tf_op jit(solution)/shard_map/update_project/pallas_call | solution.py:387
  121.7 0.0 copy-start.2
  121.8 1.1 copy-done.2
  122.9 36.2 %share_ratios.3 = f32[4,2,2,2,96,128]{5,4,3,2,1,0:T(8,128)S(1)} custom-call(f32[4,2,2,2,96,128]{5,4,3,2,1,0:T(8,128)S(1)} %bitcast.22, s32[1,96,128]{2,1,0:T(8,128)S(1)} %copy-done.3), custom_call_target="tpu_custom_call" | custom-call | tf_op jit(solution)/shard_map/share_ratios/pallas_call | solution.py:144
  159.1 16.1 %update_last.1 = f32[96,4096]{1,0:T(8,128)S(1)} custom-call(s32[35]{0:T(128)S(1)} %pad_add_fusion.meta, f32[32,8,128]{2,1,0:T(8,128)S(1)} %bitcast.21, f32[32,96,128]{2,1,0:T(8,128)S(1)} %bitcast.16, bf16[4096,4096]{1,0:T(8,128)(2,1)} %get-tuple-element.10.cover, f32[96,4096]{1,0:T(8,128)} %copy-done.2), custom_call_target="tpu_custom_call" | custom-call | tf_op jit(solution)/shard_map/update_last/pallas_call | solution.py:400
  175.2 1.6 copy.9
  (1 shorter events, 0.0 us)
Async XLA Ops:
  20.3 76.9 %copy-start = (f32[12,8,16,256]{3,1,2,0:T(8,128)}, f32[12,8,16,256]{3,1,2,0:T(8,128)S(1)}, u32[]{:S(2)}) copy-start(f32[12,8,16,256]{3,1,2,0:T(8,128)S(1)} %copy.8) | copy-start | bytes 4718596
  20.3 38.5 %copy-start.3 = (s32[1,96,128]{2,1,0:T(8,128)S(1)}, s32[1,96,128]{2,1,0:T(8,128)}, u32[]{:S(2)}) copy-start(s32[1,96,128]{2,1,0:T(8,128)} %counts.3) | copy-start | bytes 147460
  97.2 1.1 copy-start.1
  121.7 1.1 copy-start.2

commit v3 on v2

--- a/solution.py
+++ b/solution.py
@@ -9,7 +9,7 @@
 
 ITERS = 2
 GROUP = 4
-CHUNK = 512
+CHUNK = 1024
 LOG2E = 1.4426950408889634
 NT = (((1,), (1,)), ((), ()))
 VMEM = 50 << 20
@@ -213,7 +213,7 @@
         )
         return carry
 
-    lax.fori_loop(0, rows, row, 0, unroll=2)
+    lax.fori_loop(0, rows, row, 0, unroll=4)
     for s in range(GROUP):
         slot = step * GROUP + s
         value = jnp.transpose(total[s * antennas : (s + 1) * antennas, :])

time: 177 us -> 170 us (0.960)
  Pallas kernels: 167 us -> 161 us
    pallas_call x1, Pallas kernels: 38.5 us -> 33.9 us  [shards(): pl.pallas_call(cover_kernel, out_shape=(jax.ShapeDtypeStruct((slots * ant...]
where the time goes in v3:
time: 170 us
  Pallas kernels  161 us (95%)
  local copies, waits for them, and re-layouts  7.84 us (5%)
    pallas_call x3, Pallas kernels, exchange(): pl.pallas_call(functools.partial(kernel, n_row, n_col), out_shape=jax.Sha...  89.7 us
    pallas_call x1, Pallas kernels, shards(): pl.pallas_call(cover_kernel, out_shape=(jax.ShapeDtypeStruct((slots * ant...  33.9 us
    pallas_call x1, Pallas kernels, shards(): pl.pallas_call(middle_kernel, out_shape=(estimate_shape, partial_shape),...  22.6 us
    pallas_call x1, Pallas kernels, shards(): pl.pallas_call(last_kernel, out_shape=estimate_shape, grid_spec=pltpu.Pre...  14.5 us
    unnamed x11, local copies, waits for them, and re-layouts  7.1 us

profile of v3, /device:TPU:0, one launch (start us, length us, event | category | flops | bytes accessed | tf_op | source)
XLA Modules:
  0.0 170.1 jit_solution(5996501573242388284)
XLA Ops:
  0.7 0.7 pad_add_fusion.meta
  1.4 0.7 copy.7
  2.1 0.7 reshape.41.clutter
  2.8 14.9 %gather_settings.1 = f32[4,2,2,2,8,128]{5,4,3,2,1,0:T(8,128)S(1)} custom-call(f32[1,8,128]{2,1,0:T(8,128)S(1)} %pad.4.mine), custom_call_target="tpu_custom_call" | custom-call | tf_op jit(solution)/shard_map/gather_settings/pallas_call | solution.py:144
  17.8 2.5 %copy.8 = f32[12,8,16,256]{3,1,2,0:T(8,128)S(1)} copy(f32[12,8,16,256]{3,2,1,0:T(8,128)} %bitcast.24) | data formatting | bytes 3145728
  20.3 0.0 copy-start
  20.3 0.0 copy-start.3
  20.3 33.9 %cover_first.1 = (bf16[4096,4096]{1,0:T(8,128)(2,1)}, f32[32,96,128]{2,1,0:T(8,128)S(1)}) custom-call(s32[35]{0:T(128)S(1)} %pad_add_fusion.meta, f32[32,8,128]{2,1,0:T(8,128)S(1)} %bitcast.19, f32[16,1,256]{2,1,0:T(1,128)S(1)} %reshape.41.clutter, f32[96,4096]{1,0:T(8,128)S(1)} %bitcast.14), custom_call_target="tpu_custom_call" | custom-call | tf_op jit(solution)/shard_map/cover_first/pallas_call | solution.py:325
  54.2 0.0 copy-done.3
  54.2 38.4 %share_ratios.2 = f32[4,2,2,2,96,128]{5,4,3,2,1,0:T(8,128)S(1)} custom-call(f32[4,2,2,2,96,128]{5,4,3,2,1,0:T(8,128)S(1)} %bitcast.23, s32[1,96,128]{2,1,0:T(8,128)S(1)} %copy-done.3), custom_call_target="tpu_custom_call" | custom-call | tf_op jit(solution)/shard_map/share_ratios/pallas_call | solution.py:144
  92.6 0.0 copy-done
  92.6 0.0 copy-start.1
  92.6 1.1 copy-done.1
  93.8 22.6 %update_project.1 = (f32[96,4096]{1,0:T(8,128)S(1)}, f32[32,96,128]{2,1,0:T(8,128)S(1)}) custom-call(s32[35]{0:T(128)S(1)} %pad_add_fusion.meta, f32[32,8,128]{2,1,0:T(8,128)S(1)} %bitcast.20, f32[32,96,128]{2,1,0:T(8,128)} %bitcast.18, bf16[4096,4096]{1,0:T(8,128)(2,1)} %get-tuple-element.10.cover, f32[96,4096]{1,0:T(8,128)} %bitcast.15), custom_call_target="tpu_custom_call" | custom-call | tf_op jit(solution)/shard_map/update_project/pallas_call | solution.py:387
  116.4 0.0 copy-start.2
  116.4 1.1 copy-done.2
  117.6 36.3 %share_ratios.3 = f32[4,2,2,2,96,128]{5,4,3,2,1,0:T(8,128)S(1)} custom-call(f32[4,2,2,2,96,128]{5,4,3,2,1,0:T(8,128)S(1)} %bitcast.22, s32[1,96,128]{2,1,0:T(8,128)S(1)} %copy-done.3), custom_call_target="tpu_custom_call" | custom-call | tf_op jit(solution)/shard_map/share_ratios/pallas_call | solution.py:144
  153.9 14.5 %update_last.1 = f32[96,4096]{1,0:T(8,128)S(1)} custom-call(s32[35]{0:T(128)S(1)} %pad_add_fusion.meta, f32[32,8,128]{2,1,0:T(8,128)S(1)} %bitcast.21, f32[32,96,128]{2,1,0:T(8,128)S(1)} %bitcast.16, bf16[4096,4096]{1,0:T(8,128)(2,1)} %get-tuple-element.10.cover, f32[96,4096]{1,0:T(8,128)} %copy-done.2), custom_call_target="tpu_custom_call" | custom-call | tf_op jit(solution)/shard_map/update_last/pallas_call | solution.py:400
  168.5 1.6 copy.9
  (1 shorter events, 0.0 us)
Async XLA Ops:
  20.3 72.4 %copy-start = (f32[12,8,16,256]{3,1,2,0:T(8,128)}, f32[12,8,16,256]{3,1,2,0:T(8,128)S(1)}, u32[]{:S(2)}) copy-start(f32[12,8,16,256]{3,1,2,0:T(8,128)S(1)} %copy.8) | copy-start | bytes 4718596
  20.3 33.9 %copy-start.3 = (s32[1,96,128]{2,1,0:T(8,128)S(1)}, s32[1,96,128]{2,1,0:T(8,128)}, u32[]{:S(2)}) copy-start(s32[1,96,128]{2,1,0:T(8,128)} %counts.3) | copy-start | bytes 147460
  92.6 1.1 copy-start.1
  116.4 1.1 copy-start.2
